TPU v7x, 256 devices: a whole 4x4x8 slice. The times are simulated.
256 devices in a mesh: rep: 8 (over x, y_lo), fsdp: 32 (over y_hi, z, core).
Axes of the slice: x: 4, y: 4 (y_hi: 2, y_lo: 2; y = y_hi * 2 + y_lo), z: 8, core: 2. Of those that a mesh axis runs over, the one named last changes fastest.
Arguments:
- tokens: bfloat16 [4096, 4096], P('rep'), may hold values from -40 to 40
- norm_gain: float32 [4096], replicated, may hold values from 0.1 to 1.9
- gate_weight: bfloat16 [8, 4096, 7168], P('rep', None, 'fsdp'), may hold values from -6 to 6
- up_weight: bfloat16 [8, 4096, 7168], P('rep', None, 'fsdp'), may hold values from -6 to 6
- down_weight: bfloat16 [8, 7168, 4096], P('rep', 'fsdp'), may hold values from -6 to 6
- outer_block: float32 [7168, 4096], P('fsdp', 'rep'), may hold values from -6 to 6
- momentum: float32 [7168, 4096], P('fsdp', 'rep'), may hold values from -6 to 6
- cotangent: bfloat16 [4096, 4096], P('rep'), may hold values from -6 to 6
Outputs:
- mixed: bfloat16 [4096, 4096], P(('rep', 'fsdp'))
- input_grad: bfloat16 [4096, 4096], P(('rep', 'fsdp'))
- new_outer: float32 [7168, 4096], P('fsdp', 'rep')
- new_momentum: float32 [7168, 4096], P('fsdp', 'rep')
All inputs are finite; a program needn't handle non-finite values.
Results may differ from a plain program's by a relative error of at most 0.0065.
Values sent between devices are 32-bit elements; how exact they have to be, the bound alone decides.
A program may use at most 128 MiB of HBM per device.

v0:
```python
import jax
import jax.numpy as jnp
from jax import lax
from jax.sharding import PartitionSpec as P

D = 4096
FFW = 7168


def body(tokens, norm_gain, gate_weight, up_weight, down_weight, outer_block, momentum, cotangent):
    scale_in = D ** (-0.5)
    scale_out = FFW ** (-0.5)
    group_rows = tokens.shape[0]
    own_rows = group_rows // lax.axis_size("fsdp")
    first_row = lax.axis_index("fsdp") * own_rows
    gate_local = gate_weight[0]
    up_local = up_weight[0]
    down_local = down_weight[0]
    rows32 = tokens.astype(jnp.float32)
    inverse = lax.rsqrt(jnp.mean(rows32 * rows32, axis=1, keepdims=True) + 1e-05)
    plain = rows32 * inverse
    normed = (plain * norm_gain).astype(jnp.bfloat16)
    gate = jnp.dot(normed, gate_local, preferred_element_type=jnp.float32) * scale_in
    up = jnp.dot(normed, up_local, preferred_element_type=jnp.float32) * scale_in
    sig = jax.nn.sigmoid(gate)
    act = gate * sig
    hidden = (act * up).astype(jnp.bfloat16)
    mixed = lax.psum_scatter(
        jnp.dot(hidden, down_local, preferred_element_type=jnp.float32) * scale_out,
        "fsdp",
        scatter_dimension=0,
        tiled=True,
    ).astype(jnp.bfloat16)
    d_hidden = (
        lax.dot_general(
            cotangent, down_local, (((1,), (1,)), ((), ())), preferred_element_type=jnp.float32
        )
        * scale_out
    )
    grad_down = (
        lax.dot_general(
            hidden, cotangent, (((0,), (0,)), ((), ())), preferred_element_type=jnp.float32
        )
        * scale_out
    )
    d_gate = (d_hidden * up * sig * (1.0 + gate * (1.0 - sig))).astype(jnp.bfloat16)
    d_up = (d_hidden * act).astype(jnp.bfloat16)
    first = lax.dot_general(
        d_gate, gate_local, (((1,), (1,)), ((), ())), preferred_element_type=jnp.float32
    )
    second = lax.dot_general(
        d_up, up_local, (((1,), (1,)), ((), ())), preferred_element_type=jnp.float32
    )
    d_normed = lax.psum_scatter(
        (first + second) * scale_in, "fsdp", scatter_dimension=0, tiled=True
    )
    own_plain = lax.dynamic_slice_in_dim(plain, first_row, own_rows, 0)
    own_inverse = lax.dynamic_slice_in_dim(inverse, first_row, own_rows, 0)
    scaled = d_normed * norm_gain
    centre = jnp.mean(scaled * own_plain, axis=1, keepdims=True)
    input_grad = (own_inverse * (scaled - own_plain * centre)).astype(jnp.bfloat16)
    stepped = down_local.astype(jnp.float32) - 0.5 * grad_down
    replicas = lax.axis_size("rep")
    total = lax.psum(stepped, "rep")
    columns = outer_block.shape[1]
    mine = lax.dynamic_slice_in_dim(total, lax.axis_index("rep") * columns, columns, 1)
    pseudo = outer_block - mine / replicas
    new_momentum = 0.9 * momentum + pseudo
    new_outer = outer_block - 0.7 * (pseudo + 0.9 * new_momentum)
    return (mixed, input_grad, new_outer, new_momentum)


def solution(mesh):
    placed = (
        P("rep", None),
        P(),
        P("rep", None, "fsdp"),
        P("rep", None, "fsdp"),
        P("rep", "fsdp", None),
        P("fsdp", "rep"),
        P("fsdp", "rep"),
        P("rep", None),
    )
    return jax.shard_map(
        body,
        mesh=mesh,
        in_specs=placed,
        out_specs=(
            P(("rep", "fsdp"), None),
            P(("rep", "fsdp"), None),
            P("fsdp", "rep"),
            P("fsdp", "rep"),
        ),
        check_vma=False,
    )
```

profile of v0, /device:TPU:2, one launch (start us, length us, event | category | flops | bytes accessed | tf_op | source)
XLA Modules:
  0.0 395.8 jit_solution(15616865482364025231)
XLA Ops:
  8.0 0.0 copy-start
  8.0 0.0 all-reduce.2.cloned.1.call-start
  8.1 0.0 copy-start.1
  8.1 3.2 fusion
  11.3 0.3 copy-done.1
  11.6 0.0 copy-start.7
  11.6 3.1 fusion.15
  14.8 0.0 copy-done
  14.8 0.0 copy-done.7
  14.8 0.0 copy-start.2
  14.8 0.0 copy-start.3
  14.8 1.6 multiply_convert_fusion.9
  16.4 0.0 copy-done.2
  16.5 1.1 copy-done.3
  17.5 3.1 fusion.1
  20.6 0.0 all-reduce.2.cloned.1.call-update
  20.7 0.0 reduce-scatter.5.cloned.1.call-start
  20.7 0.0 copy-start.4
  20.7 4.3 %fusion.12 = f32[512,224]{0,1:T(8,128)S(1)} fusion(bf16[512,4096]{1,0:T(8,128)(2,1)} %param.15, bf16[1,224,4096]{2,1,0:T(8,128)(2,1)} %param.12), kind=kOutput, calls=%fused_computation.18 | convolution fusion | flops 939638784 | bytes 6488064 | tf_op jit(solution)/shard_map/dot_general | solution.py:35
  25.1 0.0 copy-done.4
  25.1 1.4 fusion.8
  26.5 4.7 %add_multiply_fusion = f32[512,4096]{1,0:T(8,128)} fusion(f32[512,4096]{1,0:T(8,128)S(1)} %fusion.8, bf16[1,4096,224]{1,2,0:T(8,128)(2,1)S(1)} %copy-done, f32[512,224]{0,1:T(8,128)S(1)} %fusion.12, f32[512,224]{0,1:T(8,128)S(1)} %fusion.15), kind=kOutput, calls=%fused_computation.3 | convolution fusion | flops 944406528 | bytes 19529728 | tf_op jit(solution)/shard_map/dot_general | solution.py:51
  31.2 0.0 reduce-scatter.5.cloned.1.call-update
  31.3 0.0 reduce-scatter.3.cloned.1.call-start
  31.3 6.0 %convolution_multiply_fusion = f32[512,4096]{1,0:T(8,128)} fusion(bf16[512,224]{0,1:T(8,128)(2,1)S(1)} %get-tuple-element.6, bf16[1,224,4096]{2,1,0:T(8,128)(2,1)} %param.12), kind=kOutput, calls=%fused_computation.5 | convolution fusion | flops 941621248 | bytes 10452992 | tf_op jit(solution)/shard_map/dot_general | solution.py:29
  37.3 0.0 reduce-scatter.3.cloned.1.call-update
  37.3 0.1 dynamic-slice.3
  37.4 0.0 copy-start.5
  37.4 0.0 copy-start.6
  37.4 6.7 %convert_multiply_fusion = f32[512,4096]{1,0:T(8,128)} fusion(bf16[512,4096]{1,0:T(8,128)(2,1)} %param.8, f32[512]{0:T(512)S(1)} %add_rsqrt_fusion), kind=kLoop, calls=%fused_computation | loop fusion | flops 4194304 | bytes 12584960 | tf_op jit(solution)/shard_map/mul | solution.py:21
  44.1 172.1 %all-reduce.2.cloned.1.call-done = f32[224,4096]{1,0:T(8,128)} async-done(((f32[224,4096]{1,0:T(8,128)}), f32[224,4096]{1,0:T(8,128)}) %all-reduce.2.cloned.1.call-update) | async-done | bytes 3670032 | tf_op jit(solution)/shard_map/psum | solution.py:64
  216.2 0.0 copy-done.5
  216.2 0.0 copy-done.6
  216.2 2.1 multiply_subtract_fusion
  218.3 7.2 %reduce-scatter.5.cloned.1.call-done = f32[16,4096]{1,0:T(8,128)} async-done(((f32[512,4096]{1,0:T(8,128)}), f32[16,4096]{1,0:T(8,128)}) %reduce-scatter.5.cloned.1.call-update) | async-done | bytes 262160 | tf_op jit(solution)/shard_map/reduce_scatter | solution.py:54
  225.5 1.2 multiply_reduce_fusion
  226.7 158.3 %reduce-scatter.3.cloned.1.call-done = f32[16,4096]{1,0:T(8,128)} async-done(((f32[512,4096]{1,0:T(8,128)}), f32[16,4096]{1,0:T(8,128)}) %reduce-scatter.3.cloned.1.call-update) | async-done | bytes 262160 | tf_op jit(solution)/shard_map/reduce_scatter | solution.py:28
  385.0 1.6 convert_element_type.27
  386.6 1.8 multiply_convert_fusion.10
  (2 shorter events, 0.0 us)
Async XLA Ops:
  8.0 6.8 %copy-start = (bf16[1,4096,224]{1,2,0:T(8,128)(2,1)S(1)}, bf16[1,4096,224]{1,2,0:T(8,128)(2,1)}, u32[]{:S(2)}) copy-start(bf16[1,4096,224]{1,2,0:T(8,128)(2,1)} %param.11) | copy-start | bytes 5505028
  8.0 208.2 %all-reduce.2.cloned.1.call-start = ((), (), s32[]{:S(2)}) async-start(), calls=%async_computation.4 | async-start | bytes 7340032 | tf_op jit(solution)/shard_map/psum | solution.py:64
  8.1 3.6 copy-start.1
  11.6 3.1 copy-start.7
  14.8 1.7 copy-start.2
  14.8 2.7 copy-start.3
  20.7 204.8 %reduce-scatter.5.cloned.1.call-start = ((), (), s32[]{:S(2)}) async-start(), calls=%async_computation.3 | async-start | bytes 8650752 | tf_op jit(solution)/shard_map/reduce_scatter | solution.py:54
  20.7 4.4 %copy-start.4 = (bf16[1,4096,224]{1,2,0:T(8,128)(2,1)S(1)}, bf16[1,4096,224]{1,2,0:T(8,128)(2,1)}, u32[]{:S(2)}) copy-start(bf16[1,4096,224]{1,2,0:T(8,128)(2,1)} %param.10) | copy-start | bytes 5505028
  31.3 353.7 %reduce-scatter.3.cloned.1.call-start = ((), (), s32[]{:S(2)}) async-start(), calls=%async_computation.2 | async-start | bytes 8650752 | tf_op jit(solution)/shard_map/reduce_scatter | solution.py:28
  37.4 178.8 %copy-start.5 = (f32[224,512]{1,0:T(8,128)S(1)}, f32[224,512]{1,0:T(8,128)}, u32[]{:S(2)}) copy-start(f32[224,512]{1,0:T(8,128)} %param.13) | copy-start | bytes 1376260
  37.4 178.8 %copy-start.6 = (f32[224,512]{1,0:T(8,128)S(1)}, f32[224,512]{1,0:T(8,128)}, u32[]{:S(2)}) copy-start(f32[224,512]{1,0:T(8,128)} %param.14) | copy-start | bytes 1376260
Sparse Core Ops, SparseCore 0:
  20.8 195.3 all-reduce.1
Sparse Core Ops, SparseCore 1:
  31.3 194.1 reduce-scatter.4
  229.7 155.2 reduce-scatter.2
where the time goes:
time: 396 us
  waiting for transfers between devices  338 us (85%)
  matrix products  24.3 us (6%)
  other arithmetic  16.6 us (4%)
  between operations  15.6 us (4%)
    psum x1, waiting for transfers between devices, body(): total = lax.psum(stepped, 'rep')  172 us
    reduce_scatter x1, waiting for transfers between devices, body(): lax.psum_scatter(jnp.dot(hidden, down_local, preferred_element_type=jnp.f...  158 us
  transfers between devices with their start and end apart: 3, of which 3 were waited for; matrix products, arithmetic and copies ran while one was open for 7% of the time, Pallas kernels for 0%

commit v1 on v0

v1 whole, which is shorter than its diff:
```python
import jax
import jax.numpy as jnp
from jax import lax
from jax.experimental import pallas as pl
from jax.experimental.pallas import tpu as pltpu
from jax.sharding import PartitionSpec as P

D = 4096
FFW = 7168
N_REP = 8
MESH = pl.DeviceIdType.MESH
F32 = jnp.float32
BF16 = jnp.bfloat16

NZ = 8
CA = 1280
CB = 768
A_COLS = (pl.ds(0, CA), pl.ds(CA, CA))
B_COLS = (pl.ds(2 * CA, CB), pl.ds(2 * CA + CB, CB))
A_ALL = pl.ds(0, 2 * CA)
B_ALL = pl.ds(2 * CA, 2 * CB)
SCALE_IN = D ** (-0.5)
SCALE_OUT = FFW ** (-0.5)
T0 = (((1,), (1,)), ((), ()))


def slot_of(direction, step):
    if step == NZ - 1:
        return 7
    if direction == 0:
        return 2 * step if step <= 3 else 13 - 2 * step
    return 2 * step + 1 if step <= 2 else 12 - 2 * step


OFFSETS = (-1, 1, -2, 2, -3, 3, 4, 0)


def kernel(
    tokens, gain_hbm, gate_hbm, up_hbm, down_hbm, outer_hbm, mom_hbm, cot_hbm,
    mixed_out, grad_out, outer_out, mom_out,
    tok, cot, wg, wu, wd, gain, own_tok, outer, mom,
    gate_s, up_s, hid, hid_t,
    own, peer, prec, g, arec, brec, yrec, frec, xrec, lrec,
    load_sem, tok_sem, cot_sem,
    p_sem, a_send, a_recv, b_send, b_recv, y_send, y_recv, f_sem, x_send, x_recv, l_sem,
):
    r = lax.axis_index("rep")
    f = lax.axis_index("fsdp")
    x, yl = r // 2, lax.rem(r, 2)
    yh, z, c = f // 16, lax.rem(f // 2, NZ), lax.rem(f, 2)

    def at(yh_, z_, c_):
        return (yh_ * NZ + z_) * 2 + c_

    pair = (r, at(yh, z, 1 - c))
    z_next = ((r, at(yh, lax.rem(z + 1, NZ), c)), (r, at(yh, lax.rem(z + NZ - 1, NZ), c)))
    y_peer = (r, at(1 - yh, z, c))
    x_next = ((lax.rem(x + 1, 4) * 2 + yl, f), (lax.rem(x + 3, 4) * 2 + yl, f))
    l_peer = (x * 2 + 1 - yl, f)

    barrier = pltpu.get_barrier_semaphore()
    for other in (pair, *z_next, y_peer, *x_next, l_peer):
        pl.semaphore_signal(barrier, inc=1, device_id=other, device_id_type=MESH)

    def load_rows(src, dst, sem, k):
        for h in range(2):
            for jj in range(2):
                for yp in range(2):
                    zz = lax.rem(z + OFFSETS[2 * k + jj] + NZ, NZ)
                    cc = c if h else 1 - c
                    yy = yh if yp else 1 - yh
                    row = pl.multiple_of(at(yy, zz, cc) * 16, 16)
                    pltpu.make_async_copy(
                        src.at[pl.ds(row, 16), :],
                        dst.at[pl.ds(k * 128 + h * 64 + jj * 32 + yp * 16, 16), :],
                        sem.at[k],
                    ).start()

    def wait_rows(dst, sem, k):
        block = dst.at[pl.ds(k * 128, 128), :]
        pltpu.make_async_copy(block, block, sem.at[k]).wait()

    loads = [
        pltpu.make_async_copy(gain_hbm, gain, load_sem.at[0]),
        pltpu.make_async_copy(gate_hbm.at[0], wg, load_sem.at[1]),
        pltpu.make_async_copy(up_hbm.at[0], wu, load_sem.at[2]),
        pltpu.make_async_copy(down_hbm.at[0], wd, load_sem.at[3]),
        pltpu.make_async_copy(
            tokens.at[pl.ds(pl.multiple_of(f * 16, 16), 16), :], own_tok, load_sem.at[4]
        ),
        pltpu.make_async_copy(outer_hbm, outer, load_sem.at[5]),
        pltpu.make_async_copy(mom_hbm, mom, load_sem.at[6]),
    ]
    loads[0].start()
    load_rows(tokens, tok, tok_sem, 0)
    for i in (1, 2, 3):
        loads[i].start()
    for k in (1, 2, 3):
        load_rows(tokens, tok, tok_sem, k)
    for k in range(4):
        load_rows(cot_hbm, cot, cot_sem, k)
    for i in (4, 5, 6):
        loads[i].start()

    sends = []

    def remote(src, dst, ssem, rsem, to):
        copy = pltpu.make_async_remote_copy(
            src_ref=src, dst_ref=dst, send_sem=ssem, recv_sem=rsem, device_id=to, device_id_type=MESH
        )
        copy.start()
        sends.append(copy)
        return copy

    def front(k):
        wait_rows(tok, tok_sem, k)
        if k == 0:
            loads[0].wait()

        @pl.loop(0, 8)
        def _(i):
            rows = pl.ds(pl.multiple_of(k * 128 + i * 16, 16), 16)
            part = tok[rows, :].astype(F32)
            inverse = lax.rsqrt(jnp.mean(part * part, axis=1, keepdims=True) + 1e-05)
            tok[rows, :] = (part * inverse * gain[...]).astype(BF16)

        if k == 0:
            loads[1].wait()
            loads[2].wait()
        rows = pl.ds(k * 128, 128)
        normed = tok[rows, :]
        gate = jnp.dot(normed, wg[...], preferred_element_type=F32) * SCALE_IN
        up = jnp.dot(normed, wu[...], preferred_element_type=F32) * SCALE_IN
        gate_s[rows, :] = gate
        up_s[rows, :] = up
        sig = 1.0 / (1.0 + jnp.exp(-gate))
        hid[rows, :] = (gate * sig * up).astype(BF16)

    def put(a, k, cols, value):
        peer[a, pl.ds(k * 64, 64), cols] = value[:64]
        own[a, pl.ds(k * 64, 64), cols] = value[64:]

    def mix(k):
        if k == 0:
            loads[3].wait()
        hidden = hid[pl.ds(k * 128, 128), :]

        @pl.loop(0, 8)
        def _(n):
            cols = pl.ds(pl.multiple_of(n * 512, 512), 512)
            put(0, k, cols, jnp.dot(hidden, wd[:, cols], preferred_element_type=F32))

    def back(k):
        rows = pl.ds(k * 128, 128)
        d_hidden = lax.dot_general(cot[rows, :], wd[...], T0, preferred_element_type=F32) * SCALE_OUT
        gate = gate_s[rows, :]
        up = up_s[rows, :]
        sig = 1.0 / (1.0 + jnp.exp(-gate))
        d_gate = (d_hidden * up * sig * (1.0 + gate * (1.0 - sig))).astype(BF16)
        d_up = (d_hidden * (gate * sig)).astype(BF16)

        @pl.loop(0, 8)
        def _(n):
            cols = pl.ds(pl.multiple_of(n * 512, 512), 512)
            first = lax.dot_general(d_gate, wg[cols, :], T0, preferred_element_type=F32)
            second = lax.dot_general(d_up, wu[cols, :], T0, preferred_element_type=F32)
            put(1, k, cols, first + second)

    def grad(q):
        step, side = q // 2, q % 2
        xx = lax.rem(x + 4 + (step + 1 if side else -(step + 1)), 4)
        col = pl.multiple_of((xx * 2 + (yl if side else 1 - yl)) * 512, 512)
        cols = pl.ds(col, 512)
        down_grad = jnp.dot(hid_t[...], cot[:, cols], preferred_element_type=F32)
        g[q] = wd[:, cols].astype(F32) - (0.5 * SCALE_OUT) * down_grad

    pairs, rings_a, rings_b, ys, finals, xs = {}, {}, {}, {}, {}, {}

    def pair_send(a, k):
        rows = pl.ds(k * 64, 64)
        pairs[a, k] = remote(
            peer.at[a, rows, :], prec.at[a, rows, :], p_sem.at[0, a, k], p_sem.at[1, a, k], pair
        )

    def pair_add(a, k):
        pairs[a, k].wait_recv()
        rows = pl.ds(k * 64, 64)

        @pl.loop(0, 8)
        def _(n):
            cols = pl.ds(pl.multiple_of(n * 512, 512), 512)
            own[a, rows, cols] += prec[a, rows, cols]

    def y_start(a, k):
        for j in (2 * k, 2 * k + 1):
            ys[a, j] = remote(
                own.at[a, pl.ds(j * 32, 16), B_ALL], yrec.at[a, j],
                y_send.at[a, j], y_recv.at[a, j], y_peer,
            )

    def y_add(a, k):
        for j in (2 * k, 2 * k + 1):
            ys[a, j].wait_recv()
            own[a, pl.ds(j * 32 + 16, 16), B_ALL] += yrec[a, j]

    def ring_a(a, step):
        for d in range(2):
            rows = pl.ds(slot_of(d, step) * 32, 32)
            if step:
                rings_a[a, d, step - 1].wait_recv()
                own[a, rows, A_COLS[d]] += arec[a, d, step - 1]
            if step < NZ - 1:
                rings_a[a, d, step] = remote(
                    own.at[a, rows, A_COLS[d]], arec.at[a, d, step],
                    a_send.at[a, d, step], a_recv.at[a, d, step], z_next[d],
                )

    def ring_b(a, step):
        for d in range(2):
            rows = pl.ds(slot_of(d, step) * 32 + 16, 16)
            if step:
                rings_b[a, d, step - 1].wait_recv()
                own[a, rows, B_COLS[d]] += brec[a, d, step - 1]
            if step < NZ - 1:
                rings_b[a, d, step] = remote(
                    own.at[a, rows, B_COLS[d]], brec.at[a, d, step],
                    b_send.at[a, d, step], b_recv.at[a, d, step], z_next[d],
                )

    def final_start(a):
        ring_a(a, NZ - 1)
        finals[a] = remote(
            own.at[a, pl.ds(224, 16), A_ALL], frec.at[a], f_sem.at[0, a], f_sem.at[1, a], y_peer
        )

    def final_add(a):
        finals[a].wait_recv()
        own[a, pl.ds(240, 16), A_ALL] += frec[a]

    def x_step(step):
        for d in range(2):
            if step:
                xs[d, step - 1].wait_recv()
                g[2 * step + d] += xrec[d, step - 1]
            if step < 3:
                xs[d, step] = remote(
                    g.at[2 * step + d], xrec.at[d, step], x_send.at[d, step], x_recv.at[d, step], x_next[d]
                )
        if step == 3:
            xs["l"] = remote(g.at[6], lrec, l_sem.at[0], l_sem.at[1], l_peer)

    front(0)
    pl.semaphore_wait(barrier, 7)
    mix(0)
    pair_send(0, 0)
    front(1)
    pair_add(0, 0)
    ring_a(0, 0)
    y_start(0, 0)
    mix(1)
    pair_send(0, 1)
    front(2)
    pair_add(0, 1)
    ring_a(0, 1)
    y_start(0, 1)
    y_add(0, 0)
    ring_b(0, 0)
    mix(2)
    pair_send(0, 2)
    front(3)
    pair_add(0, 2)
    ring_a(0, 2)
    y_start(0, 2)
    y_add(0, 1)
    ring_b(0, 1)
    mix(3)
    pair_send(0, 3)
    hid_t[...] = hid[...].T
    for k in range(4):
        wait_rows(cot, cot_sem, k)
    grad(0)
    grad(1)
    x_step(0)
    pair_add(0, 3)
    ring_a(0, 3)
    y_start(0, 3)
    y_add(0, 2)
    ring_b(0, 2)
    for q in range(2, 8):
        grad(q)
    back(0)
    pair_send(1, 0)
    ring_a(0, 4)
    y_add(0, 3)
    ring_b(0, 3)
    back(1)
    pair_send(1, 1)
    pair_add(1, 0)
    ring_a(1, 0)
    y_start(1, 0)
    ring_a(0, 5)
    ring_b(0, 4)
    x_step(1)
    back(2)
    pair_send(1, 2)
    pair_add(1, 1)
    ring_a(1, 1)
    y_start(1, 1)
    ring_a(0, 6)
    ring_b(0, 5)
    y_add(1, 0)
    ring_b(1, 0)
    back(3)
    pair_send(1, 3)
    pair_add(1, 2)
    ring_a(1, 2)
    y_start(1, 2)
    final_start(0)
    ring_b(0, 6)
    y_add(1, 1)
    ring_b(1, 1)
    x_step(2)
    pair_add(1, 3)
    ring_a(1, 3)
    y_start(1, 3)
    ring_b(0, 7)
    y_add(1, 2)
    ring_b(1, 2)
    final_add(0)
    mixed_out[...] = (own[0, pl.ds(240, 16), :] * SCALE_OUT).astype(BF16)
    ring_a(1, 4)
    y_add(1, 3)
    ring_b(1, 3)
    x_step(3)
    ring_a(1, 5)
    ring_b(1, 4)
    ring_a(1, 6)
    ring_b(1, 5)
    final_start(1)
    ring_b(1, 6)
    ring_b(1, 7)
    final_add(1)

    loads[4].wait()
    part = own_tok[...].astype(F32)
    inverse = lax.rsqrt(jnp.mean(part * part, axis=1, keepdims=True) + 1e-05)
    plain = part * inverse
    scaled = own[1, pl.ds(240, 16), :] * SCALE_IN * gain[...]
    centre = jnp.mean(scaled * plain, axis=1, keepdims=True)
    grad_out[...] = (inverse * (scaled - plain * centre)).astype(BF16)

    loads[5].wait()
    loads[6].wait()
    xs["l"].wait_recv()
    total = g[7] + lrec[...]
    pseudo = outer[...] - total * (1.0 / N_REP)
    new_momentum = 0.9 * mom[...] + pseudo
    mom_out[...] = new_momentum
    outer_out[...] = outer[...] - 0.7 * (pseudo + 0.9 * new_momentum)

    for copy in sends:
        copy.wait_send()


def body(tokens, norm_gain, gate_weight, up_weight, down_weight, outer_block, momentum, cotangent):
    units = down_weight.shape[1]
    cols = outer_block.shape[1]
    hbm = pl.BlockSpec(memory_space=pl.ANY)
    vmem = pl.BlockSpec(memory_space=pltpu.VMEM)
    dma = pltpu.SemaphoreType.DMA
    v = pltpu.VMEM
    return pl.pallas_call(
        kernel,
        name="window",
        out_shape=(
            jax.ShapeDtypeStruct((16, D), BF16),
            jax.ShapeDtypeStruct((16, D), BF16),
            jax.ShapeDtypeStruct((units, cols), F32),
            jax.ShapeDtypeStruct((units, cols), F32),
        ),
        in_specs=[hbm] * 8,
        out_specs=(vmem,) * 4,
        scratch_shapes=[
            v((512, D), BF16), v((512, D), BF16), v((D, units), BF16), v((D, units), BF16),
            v((units, D), BF16), v((1, D), F32), v((16, D), BF16), v((units, cols), F32), v((units, cols), F32),
            v((512, units), F32), v((512, units), F32), v((512, units), BF16), v((units, 512), BF16),
            v((2, 256, D), F32), v((2, 256, D), F32), v((2, 256, D), F32), v((8, units, cols), F32),
            v((2, 2, 7, 32, CA), F32), v((2, 2, 7, 16, CB), F32), v((2, 8, 16, 2 * CB), F32),
            v((2, 16, 2 * CA), F32), v((2, 3, units, cols), F32), v((units, cols), F32),
            dma((7,)), dma((4,)), dma((4,)),
            dma((2, 2, 4)), dma((2, 2, 7)), dma((2, 2, 7)), dma((2, 2, 7)), dma((2, 2, 7)),
            dma((2, 8)), dma((2, 8)), dma((2, 2)), dma((2, 3)), dma((2, 3)), dma((2,)),
        ],
        compiler_params=pltpu.CompilerParams(
            collective_id=0, has_side_effects=True, vmem_limit_bytes=63 * 2**20
        ),
    )(tokens, norm_gain.reshape(1, D), gate_weight, up_weight, down_weight, outer_block, momentum, cotangent)


def solution(mesh):
    placed = (
        P("rep", None),
        P(),
        P("rep", None, "fsdp"),
        P("rep", None, "fsdp"),
        P("rep", "fsdp", None),
        P("fsdp", "rep"),
        P("fsdp", "rep"),
        P("rep", None),
    )
    return jax.shard_map(
        body,
        mesh=mesh,
        in_specs=placed,
        out_specs=(
            P(("rep", "fsdp"), None),
            P(("rep", "fsdp"), None),
            P("fsdp", "rep"),
            P("fsdp", "rep"),
        ),
        check_vma=False,
    )
```

time: 396 us -> 110 us (0.28)
  waiting for transfers between devices: 338 us -> 0 us
  Pallas kernels: 0 us -> 95.5 us
  matrix products: 24.3 us -> 0 us
  other arithmetic: 16.6 us -> 0 us
  between operations: 15.6 us -> 0.65 us
  local copies, waits for them, and re-layouts: 1.52 us -> 13.4 us
    psum x1 -> x0, waiting for transfers between devices: 172 us -> none  [body(): total = lax.psum(stepped, 'rep')]
    reduce_scatter x2 -> x0, waiting for transfers between devices: 165 us -> none  [the longest x1 158 us: body(): lax.psum_scatter(jnp.dot(hidden, down_local, preferred_element_type=jnp.f...]
    pallas_call x0 -> x1, Pallas kernels: none -> 95.5 us  [body(): pl.pallas_call(kernel, name='window', out_shape=(jax.ShapeDtypeStruct((16...]
    dot_general x7 -> x0, matrix products: 24.3 us -> none  [the longest x1 6.01 us: body(): jnp.dot(hidden, down_local, preferred_element_type=jnp.float32) * scale_out]
    unnamed x16 -> x8, local copies, waits for them, and re-layouts: 1.44 us -> 13.4 us
    mul x1 -> x0, other arithmetic: 6.66 us -> none  [body(): plain = rows32 * inverse]
    reduce_sum x2 -> x0, other arithmetic: 4.41 us -> none  [the longest x1 3.23 us: body(): jnp.mean(rows32 * rows32, axis=1, keepdims=True) + 1e-05]
  transfers between devices with their start and end apart: 3 -> 0, of which waited for: 3 -> 0; matrix products, arithmetic and copies ran while one was open for 7% -> 0% of each run, Pallas kernels for 0% -> 0%
where the time goes in v1:
time: 110 us; the launch traced here: 109 us
  Pallas kernels  95.5 us (87%)
  local copies, waits for them, and re-layouts  13.4 us (12%)
    pallas_call x1, Pallas kernels, body(): pl.pallas_call(kernel, name='window', out_shape=(jax.ShapeDtypeStruct((16...  95.5 us
    unnamed x8, local copies, waits for them, and re-layouts  13.4 us

profile of v1, /device:TPU:2, one launch (start us, length us, event | category | flops | bytes accessed | tf_op | source)
XLA Modules:
  0.0 109.5 jit_solution(18333729549060137025)
XLA Ops:
  0.6 0.0 copy-start
  0.6 4.1 %copy.12.gate_hbm = bf16[1,4096,224]{2,1,0:T(8,128)(2,1)} copy(bf16[1,4096,224]{1,2,0:T(8,128)(2,1)} %param.10) | data formatting | bytes 3670016 | tf_op args[2]
  4.8 0.0 copy-done
  4.8 2.5 %copy.13.up_hbm = bf16[1,4096,224]{2,1,0:T(8,128)(2,1)} copy(bf16[1,4096,224]{1,2,0:T(8,128)(2,1)S(1)} %copy-done) | data formatting | bytes 3670016 | tf_op args[3]
  7.2 95.5 %window.1 = (bf16[16,4096]{1,0:T(8,128)(2,1)}, bf16[16,4096]{1,0:T(8,128)(2,1)}, f32[224,512]{1,0:T(8,128)}, f32[224,512]{1,0:T(8,128)}) custom-call(bf16[512,4096]{1,0:T(8,128)(2,1)} %tokens.1, f32[1,4096]{1,0:T(1,128)} %bitcast.1, bf16[1,4096,224]{2,1,0:T(8,128)(2,1)} %copy.12.gate_hbm, bf16[1,4096,224]{2,1,0:T(8,128)(2,1)} %copy.13.up_hbm, ...), custom_call_target="tpu_custom_call" | custom-call | tf_op jit(solution)/shard_map/window/pallas_call | solution.py:372
  102.7 1.6 %copy.18 = bf16[16,4096]{1,0:T(8,128)(2,1)} copy(bf16[16,4096]{1,0:T(8,128)(2,1)} %get-tuple-element.8) | data formatting | bytes 262144
  104.3 1.6 %copy.19 = bf16[16,4096]{1,0:T(8,128)(2,1)} copy(bf16[16,4096]{1,0:T(8,128)(2,1)} %get-tuple-element.9) | data formatting | bytes 262144
  105.8 1.8 %copy.20 = f32[224,512]{1,0:T(8,128)} copy(f32[224,512]{1,0:T(8,128)} %get-tuple-element.10) | data formatting | bytes 917504
  107.7 1.8 %copy.21 = f32[224,512]{1,0:T(8,128)} copy(f32[224,512]{1,0:T(8,128)} %get-tuple-element.11) | data formatting | bytes 917504
Async XLA Ops:
  0.6 4.1 %copy-start = (bf16[1,4096,224]{1,2,0:T(8,128)(2,1)S(1)}, bf16[1,4096,224]{1,2,0:T(8,128)(2,1)}, u32[]{:S(2)}) copy-start(bf16[1,4096,224]{1,2,0:T(8,128)(2,1)} %param.11) | copy-start | bytes 5505028

commit v2 on v1

v2 whole, which is shorter than its diff:
```python
import jax
import jax.numpy as jnp
from jax import lax
from jax.experimental import pallas as pl
from jax.experimental.pallas import tpu as pltpu
from jax.sharding import PartitionSpec as P

D = 4096
FFW = 7168
N_REP = 8
MESH = pl.DeviceIdType.MESH
F32 = jnp.float32
BF16 = jnp.bfloat16

NZ = 8
CA = (1152, 768)
CB = (896, 1280)
SCALE_IN = D ** (-0.5)
SCALE_OUT = FFW ** (-0.5)
NT = (((1,), (1,)), ((), ()))
OFFSETS = (-1, 1, -2, 2, -3, 3, 4, 0)


def groups(a):
    return ((0, CA[a]), (CA[a], CA[a]), (2 * CA[a], CB[a]), (2 * CA[a] + CB[a], CB[a]))


def pieces(start, size):
    return [(start + i, min(512, size - i)) for i in range(0, size, 512)]


def slot_of(direction, step):
    if step == NZ - 1:
        return 7
    if direction == 0:
        return 2 * step if step <= 3 else 13 - 2 * step
    return 2 * step + 1 if step <= 2 else 12 - 2 * step


def kernel(
    tokens, gain_hbm, gate_hbm, up_hbm, down_hbm, outer_hbm, mom_hbm, cot_hbm,
    mixed_out, grad_out, outer_out, mom_out,
    tok, cot, wg, wu, wd, gain, own_tok, outer, mom, mixed_v, grad_v,
    gate_s, up_s, hid, hid_t,
    own, peer, prec, g, arec0, arec1, brec0, brec1, yrec0, yrec1, frec0, frec1, xrec, lrec,
    load_sem, tok_sem, cot_sem, out_sem,
    p_send, p_recv, a_send, a_recv, b_send, b_recv, y_send, y_recv, f_sem, x_send, x_recv, l_sem,
):
    arec, brec, yrec, frec = (arec0, arec1), (brec0, brec1), (yrec0, yrec1), (frec0, frec1)
    r = lax.axis_index("rep")
    f = lax.axis_index("fsdp")
    x, yl = r // 2, lax.rem(r, 2)
    yh, z, c = f // 16, lax.rem(f // 2, NZ), lax.rem(f, 2)

    def at(yh_, z_, c_):
        return (yh_ * NZ + z_) * 2 + c_

    pair = (r, at(yh, z, 1 - c))
    z_next = ((r, at(yh, lax.rem(z + 1, NZ), c)), (r, at(yh, lax.rem(z + NZ - 1, NZ), c)))
    y_peer = (r, at(1 - yh, z, c))
    x_next = ((lax.rem(x + 1, 4) * 2 + yl, f), (lax.rem(x + 3, 4) * 2 + yl, f))
    l_peer = (x * 2 + 1 - yl, f)

    def load_rows(src, dst, sem, k):
        for h in range(2):
            for jj in range(2):
                for yp in range(2):
                    zz = lax.rem(z + OFFSETS[2 * k + jj] + NZ, NZ)
                    cc = c if h else 1 - c
                    yy = yh if yp else 1 - yh
                    row = pl.multiple_of(at(yy, zz, cc) * 16, 16)
                    pltpu.make_async_copy(
                        src.at[pl.ds(row, 16), :],
                        dst.at[pl.ds(k * 128 + h * 64 + jj * 32 + yp * 16, 16), :],
                        sem.at[k],
                    ).start()

    def wait_rows(dst, sem, k):
        block = dst.at[pl.ds(k * 128, 128), :]
        pltpu.make_async_copy(block, block, sem.at[k]).wait()

    loads = [
        pltpu.make_async_copy(gain_hbm, gain, load_sem.at[0]),
        pltpu.make_async_copy(gate_hbm.at[0], wg, load_sem.at[1]),
        pltpu.make_async_copy(up_hbm.at[0], wu, load_sem.at[2]),
        pltpu.make_async_copy(down_hbm.at[0], wd, load_sem.at[3]),
        pltpu.make_async_copy(
            tokens.at[pl.ds(pl.multiple_of(f * 16, 16), 16), :], own_tok, load_sem.at[4]
        ),
        pltpu.make_async_copy(outer_hbm, outer, load_sem.at[5]),
        pltpu.make_async_copy(mom_hbm, mom, load_sem.at[6]),
    ]
    loads[0].start()
    load_rows(tokens, tok, tok_sem, 0)
    for i in (1, 2):
        loads[i].start()

    barrier = pltpu.get_barrier_semaphore()
    for other in (pair, *z_next, y_peer, *x_next, l_peer):
        pl.semaphore_signal(barrier, inc=1, device_id=other, device_id_type=MESH)

    loads[3].start()
    load_rows(tokens, tok, tok_sem, 1)
    load_rows(cot_hbm, cot, cot_sem, 0)
    for k in (2, 3):
        load_rows(tokens, tok, tok_sem, k)
    for k in (1, 2, 3):
        load_rows(cot_hbm, cot, cot_sem, k)
    for i in (4, 5, 6):
        loads[i].start()

    sends = []
    drained = [0]

    def remote(src, dst, ssem, rsem, to):
        copy = pltpu.make_async_remote_copy(
            src_ref=src, dst_ref=dst, send_sem=ssem, recv_sem=rsem, device_id=to, device_id_type=MESH
        )
        copy.start()
        sends.append(copy)
        return copy

    def drain(keep=16):
        until = max(drained[0], len(sends) - keep)
        for copy in sends[drained[0] : until]:
            copy.wait_send()
        drained[0] = until

    pairs, rings_a, rings_b, ys, finals, xs = {}, {}, {}, {}, {}, {}

    def pair_send(a, k, i):
        where = (a, pl.ds(k * 64, 64), pl.ds(*groups(a)[i]))
        pairs[a, k, i] = remote(
            peer.at[where], prec.at[where], p_send.at[a, k, i], p_recv.at[a, k, i], pair
        )

    def pair_add(a, k):
        for i in range(4):
            pairs[a, k, i].wait_recv()
            where = (a, pl.ds(k * 64, 64), pl.ds(*groups(a)[i]))
            own[where] += prec[where]

    def y_start(a, k):
        cols = pl.ds(2 * CA[a], 2 * CB[a])
        for j in (2 * k, 2 * k + 1):
            ys[a, j] = remote(
                own.at[a, pl.ds(j * 32, 16), cols], yrec[a].at[j],
                y_send.at[a, j], y_recv.at[a, j], y_peer,
            )

    def y_add(a, k):
        cols = pl.ds(2 * CA[a], 2 * CB[a])
        for j in (2 * k, 2 * k + 1):
            ys[a, j].wait_recv()
            own[a, pl.ds(j * 32 + 16, 16), cols] += yrec[a][j]

    def ring_a(a, step):
        for d in range(2):
            where = (a, pl.ds(slot_of(d, step) * 32, 32), pl.ds(*groups(a)[d]))
            if step:
                rings_a[a, d, step - 1].wait_recv()
                own[where] += arec[a][d, step - 1]
            if step < NZ - 1:
                rings_a[a, d, step] = remote(
                    own.at[where], arec[a].at[d, step], a_send.at[a, d, step], a_recv.at[a, d, step], z_next[d]
                )

    def ring_b(a, step):
        for d in range(2):
            where = (a, pl.ds(slot_of(d, step) * 32 + 16, 16), pl.ds(*groups(a)[2 + d]))
            if step:
                rings_b[a, d, step - 1].wait_recv()
                own[where] += brec[a][d, step - 1]
            if step < NZ - 1:
                rings_b[a, d, step] = remote(
                    own.at[where], brec[a].at[d, step], b_send.at[a, d, step], b_recv.at[a, d, step], z_next[d]
                )

    def final_start(a):
        ring_a(a, NZ - 1)
        finals[a] = remote(
            own.at[a, pl.ds(224, 16), pl.ds(0, 2 * CA[a])], frec[a], f_sem.at[0, a], f_sem.at[1, a], y_peer
        )

    def final_add(a):
        finals[a].wait_recv()
        own[a, pl.ds(240, 16), pl.ds(0, 2 * CA[a])] += frec[a][...]
        if a == 0:
            mixed_v[...] = (own[0, pl.ds(240, 16), :] * SCALE_OUT).astype(BF16)
            stores[0].start()

    def x_step(step):
        for d in range(2):
            if step:
                xs[d, step - 1].wait_recv()
                g[2 * step + d] += xrec[d, step - 1]
            if step < 3:
                xs[d, step] = remote(
                    g.at[2 * step + d], xrec.at[d, step], x_send.at[d, step], x_recv.at[d, step], x_next[d]
                )
        if step == 3:
            xs["l"] = remote(g.at[6], lrec, l_sem.at[0], l_sem.at[1], l_peer)

    def l_add():
        loads[5].wait()
        loads[6].wait()
        xs["l"].wait_recv()
        total = g[7] + lrec[...]
        held = outer[...]
        pseudo = held - total * (1.0 / N_REP)
        new_momentum = 0.9 * mom[...] + pseudo
        mom[...] = new_momentum
        outer[...] = held - 0.7 * (pseudo + 0.9 * new_momentum)
        stores[2].start()
        stores[3].start()

    stores = [
        pltpu.make_async_copy(mixed_v, mixed_out, out_sem.at[0]),
        pltpu.make_async_copy(grad_v, grad_out, out_sem.at[1]),
        pltpu.make_async_copy(outer, outer_out, out_sem.at[2]),
        pltpu.make_async_copy(mom, mom_out, out_sem.at[3]),
    ]

    def norm(k):
        wait_rows(tok, tok_sem, k)
        if k == 0:
            loads[0].wait()

        def some(i, carry):
            rows = pl.ds(pl.multiple_of(k * 128 + i * 16, 16), 16)
            part = tok[rows, :].astype(F32)
            inverse = lax.rsqrt(jnp.mean(part * part, axis=1, keepdims=True) + 1e-05)
            tok[rows, :] = (part * inverse * gain[...]).astype(BF16)
            return carry

        lax.fori_loop(0, 8, some, 0, unroll=2)

    def front(k):
        if k == 0:
            loads[1].wait()
            loads[2].wait()
        rows = pl.ds(k * 128, 128)
        normed = tok[rows, :]
        gate = lax.dot_general(normed, wg[...], NT, preferred_element_type=F32) * SCALE_IN
        up = lax.dot_general(normed, wu[...], NT, preferred_element_type=F32) * SCALE_IN
        gate_s[rows, :] = gate
        up_s[rows, :] = up
        sig = 1.0 / (1.0 + jnp.exp(-gate))
        hid[rows, :] = (gate * sig * up).astype(BF16)

    def put(a, k, value_of):
        for i, group in enumerate(groups(a)):
            for start, size in pieces(*group):
                cols = pl.ds(start, size)
                value = value_of(cols)
                peer[a, pl.ds(k * 64, 64), cols] = value[:64]
                own[a, pl.ds(k * 64, 64), cols] = value[64:]
            pair_send(a, k, i)

    def mix(k):
        if k == 0:
            loads[3].wait()
        hidden = hid[pl.ds(k * 128, 128), :]
        put(0, k, lambda cols: jnp.dot(hidden, wd[:, cols], preferred_element_type=F32))

    waited = set()

    def need_cot(k):
        if k not in waited:
            waited.add(k)
            wait_rows(cot, cot_sem, k)

    def back(k):
        need_cot(k)
        rows = pl.ds(k * 128, 128)
        d_hidden = lax.dot_general(cot[rows, :], wd[...], NT, preferred_element_type=F32) * SCALE_OUT
        gate = gate_s[rows, :]
        up = up_s[rows, :]
        sig = 1.0 / (1.0 + jnp.exp(-gate))
        d_gate = (d_hidden * up * sig * (1.0 + gate * (1.0 - sig))).astype(BF16)
        d_up = (d_hidden * (gate * sig)).astype(BF16)
        put(
            1, k,
            lambda cols: jnp.dot(d_gate, wg[:, cols], preferred_element_type=F32)
            + jnp.dot(d_up, wu[:, cols], preferred_element_type=F32),
        )

    def grad(q):
        if q == 0:
            hid_t[...] = hid[...].T
            for k in range(4):
                need_cot(k)
        step, side = q // 2, q % 2
        xx = lax.rem(x + 4 + (step + 1 if side else -(step + 1)), 4)
        col = pl.multiple_of((xx * 2 + (yl if side else 1 - yl)) * 512, 512)
        cols = pl.ds(col, 512)
        down_grad = jnp.dot(hid_t[...], cot[:, cols], preferred_element_type=F32)
        g[q] = wd[:, cols].astype(F32) - (0.5 * SCALE_OUT) * down_grad

    norm(0)
    front(0)
    pl.semaphore_wait(barrier, 7)
    mix(0)
    back(0)
    pair_add(0, 0)
    y_start(0, 0)
    ring_a(0, 0)
    norm(1)
    pair_add(1, 0)
    y_start(1, 0)
    ring_a(1, 0)
    front(1)
    mix(1)
    norm(2)
    norm(3)
    pair_add(0, 1)
    y_start(0, 1)
    ring_a(0, 1)
    y_add(0, 0)
    ring_b(0, 0)
    front(2)
    mix(2)
    front(3)
    pair_add(0, 2)
    ring_a(0, 2)
    y_start(0, 2)
    y_add(1, 0)
    ring_b(1, 0)
    mix(3)
    grad(0)
    grad(1)
    x_step(0)
    grad(2)
    grad(3)
    grad(4)
    grad(5)
    pair_add(0, 3)
    y_start(0, 3)
    ring_a(0, 3)
    y_add(0, 1)
    ring_b(0, 1)
    grad(6)
    grad(7)
    back(1)
    ring_a(0, 4)
    y_add(0, 2)
    pair_add(1, 1)
    y_start(1, 1)
    ring_b(0, 2)
    ring_a(1, 1)
    back(2)
    x_step(1)
    ring_a(0, 5)
    y_add(0, 3)
    ring_b(0, 3)
    pair_add(1, 2)
    y_start(1, 2)
    back(3)
    ring_a(1, 2)
    ring_a(0, 6)
    pair_add(1, 3)
    y_start(1, 3)
    ring_b(0, 4)
    y_add(1, 1)
    ring_b(1, 1)
    ring_a(1, 3)
    x_step(2)
    final_start(0)
    ring_b(0, 5)
    y_add(1, 2)
    ring_b(1, 2)
    drain()
    ring_a(1, 4)
    ring_b(0, 6)
    y_add(1, 3)
    ring_b(1, 3)
    drain()
    ring_a(1, 5)
    x_step(3)
    ring_b(0, 7)
    final_add(0)
    ring_b(1, 4)
    drain()
    ring_a(1, 6)
    ring_b(1, 5)
    drain()
    final_start(1)
    ring_b(1, 6)
    l_add()
    ring_b(1, 7)
    drain()
    final_add(1)

    loads[4].wait()
    part = own_tok[...].astype(F32)
    inverse = lax.rsqrt(jnp.mean(part * part, axis=1, keepdims=True) + 1e-05)
    plain = part * inverse
    scaled = own[1, pl.ds(240, 16), :] * SCALE_IN * gain[...]
    centre = jnp.mean(scaled * plain, axis=1, keepdims=True)
    grad_v[...] = (inverse * (scaled - plain * centre)).astype(BF16)
    stores[1].start()
    drain(0)
    for store in stores:
        store.wait()


def hand_on(*refs):
    held, sem = refs[8:12], refs[12]
    into = [pltpu.make_async_copy(refs[i], held[i], sem.at[0, i]) for i in range(4)]
    out = [pltpu.make_async_copy(held[i], refs[i + 4], sem.at[1, i]) for i in range(4)]
    for copy in into:
        copy.start()
    for i in range(4):
        into[i].wait()
        out[i].start()
    for copy in out:
        copy.wait()


def body(tokens, norm_gain, gate_weight, up_weight, down_weight, outer_block, momentum, cotangent):
    units = down_weight.shape[1]
    cols = outer_block.shape[1]
    hbm = pl.BlockSpec(memory_space=pl.ANY)
    dma = pltpu.SemaphoreType.DMA
    v = pltpu.VMEM
    results = (
        jax.ShapeDtypeStruct((16, D), BF16),
        jax.ShapeDtypeStruct((16, D), BF16),
        jax.ShapeDtypeStruct((units, cols), F32),
        jax.ShapeDtypeStruct((units, cols), F32),
    )
    made = pl.pallas_call(
        kernel,
        name="window",
        out_shape=results,
        in_specs=[hbm] * 8,
        out_specs=(hbm,) * 4,
        scratch_shapes=[
            v((512, D), BF16), v((512, D), BF16), v((units, D), BF16), v((units, D), BF16),
            v((units, D), BF16), v((1, D), F32), v((16, D), BF16), v((units, cols), F32), v((units, cols), F32),
            v((16, D), BF16), v((16, D), BF16),
            v((512, units), F32), v((512, units), F32), v((512, units), BF16), v((units, 512), BF16),
            v((2, 256, D), F32), v((2, 256, D), F32), v((2, 256, D), F32), v((8, units, cols), F32),
            v((2, 7, 32, CA[0]), F32), v((2, 7, 32, CA[1]), F32),
            v((2, 7, 16, CB[0]), F32), v((2, 7, 16, CB[1]), F32),
            v((8, 16, 2 * CB[0]), F32), v((8, 16, 2 * CB[1]), F32),
            v((16, 2 * CA[0]), F32), v((16, 2 * CA[1]), F32),
            v((2, 3, units, cols), F32), v((units, cols), F32),
            dma((7,)), dma((4,)), dma((4,)), dma((4,)),
            dma((2, 4, 4)), dma((2, 4, 4)), dma((2, 2, 7)), dma((2, 2, 7)), dma((2, 2, 7)), dma((2, 2, 7)),
            dma((2, 8)), dma((2, 8)), dma((2, 2)), dma((2, 3)), dma((2, 3)), dma((2,)),
        ],
        compiler_params=pltpu.CompilerParams(
            collective_id=0, has_side_effects=True, vmem_limit_bytes=63 * 2**20
        ),
    )(
        tokens, norm_gain.reshape(1, D), jnp.swapaxes(gate_weight, 1, 2), jnp.swapaxes(up_weight, 1, 2),
        down_weight, outer_block, momentum, cotangent,
    )
    return pl.pallas_call(
        hand_on,
        name="hand_on",
        out_shape=results,
        in_specs=[hbm] * 4,
        out_specs=(hbm,) * 4,
        scratch_shapes=[v(result.shape, result.dtype) for result in results] + [dma((2, 4))],
    )(*made)


def solution(mesh):
    placed = (
        P("rep", None),
        P(),
        P("rep", None, "fsdp"),
        P("rep", None, "fsdp"),
        P("rep", "fsdp", None),
        P("fsdp", "rep"),
        P("fsdp", "rep"),
        P("rep", None),
    )
    return jax.shard_map(
        body,
        mesh=mesh,
        in_specs=placed,
        out_specs=(
            P(("rep", "fsdp"), None),
            P(("rep", "fsdp"), None),
            P("fsdp", "rep"),
            P("fsdp", "rep"),
        ),
        check_vma=False,
    )
```

time: 110 us -> 88 us (0.80)
  local copies, waits for them, and re-layouts: 13.4 us -> 0 us
  Pallas kernels: 95.5 us -> 87.1 us
    unnamed x8 -> x0, local copies, waits for them, and re-layouts: 13.4 us -> none
    pallas_call x1 -> x2, Pallas kernels: 95.5 us -> 87.1 us  [the longest x1 85 us: body(): pl.pallas_call(kernel, name='window', out_shape=results, in_specs=[hbm] *...]
where the time goes in v2:
time: 88 us; the launch traced here: 87.9 us
  Pallas kernels  87.1 us (99%)
    pallas_call x1, Pallas kernels, body(): pl.pallas_call(kernel, name='window', out_shape=results, in_specs=[hbm] *...  85 us
    pallas_call x1, Pallas kernels, body(): pl.pallas_call(hand_on, name='hand_on', out_shape=results, in_specs=[hbm]...  2.14 us

profile of v2, /device:TPU:2, one launch (start us, length us, event | category | flops | bytes accessed | tf_op | source)
XLA Modules:
  0.0 87.9 jit_solution(10973054088425535681)
XLA Ops:
  0.6 85.0 %window.1 = (bf16[16,4096]{1,0:T(8,128)(2,1)}, bf16[16,4096]{1,0:T(8,128)(2,1)}, f32[224,512]{1,0:T(8,128)}, f32[224,512]{1,0:T(8,128)}) custom-call(bf16[512,4096]{1,0:T(8,128)(2,1)} %tokens.1, f32[1,4096]{1,0:T(1,128)} %bitcast.5, bf16[1,224,4096]{2,1,0:T(8,128)(2,1)} %bitcast.3, bf16[1,224,4096]{2,1,0:T(8,128)(2,1)} %bitcast.4, ...), custom_call_target="tpu_custom_call" | custom-call | tf_op jit(solution)/shard_map/window/pallas_call | solution.py:432
  85.6 2.1 %hand_on.1 = (bf16[16,4096]{1,0:T(8,128)(2,1)}, bf16[16,4096]{1,0:T(8,128)(2,1)}, f32[224,512]{1,0:T(8,128)}, f32[224,512]{1,0:T(8,128)}) custom-call(bf16[16,4096]{1,0:T(8,128)(2,1)} %get-tuple-element.8.refs_0_, bf16[16,4096]{1,0:T(8,128)(2,1)} %get-tuple-element.9.refs_1_, f32[224,512]{1,0:T(8,128)} %get-tuple-element.10.refs_2_, ...), custom_call_target="tpu_custom_call" | custom-call | tf_op jit(solution)/shard_map/hand_on/pallas_call | solution.py:460

commit v3 on v2

--- a/solution.py
+++ b/solution.py
@@ -13,8 +13,8 @@
 BF16 = jnp.bfloat16
 
 NZ = 8
-CA = (1152, 768)
-CB = (896, 1280)
+CA = (1024, 1024)
+CB = (1024, 1024)
 SCALE_IN = D ** (-0.5)
 SCALE_OUT = FFW ** (-0.5)
 NT = (((1,), (1,)), ((), ()))
@@ -140,19 +140,12 @@
             where = (a, pl.ds(k * 64, 64), pl.ds(*groups(a)[i]))
             own[where] += prec[where]
 
-    def y_start(a, k):
-        cols = pl.ds(2 * CA[a], 2 * CB[a])
-        for j in (2 * k, 2 * k + 1):
-            ys[a, j] = remote(
-                own.at[a, pl.ds(j * 32, 16), cols], yrec[a].at[j],
-                y_send.at[a, j], y_recv.at[a, j], y_peer,
+    def y_start(a, step):
+        for d in range(2):
+            ys[a, d, step] = remote(
+                own.at[a, pl.ds(slot_of(d, step) * 32, 16), pl.ds(*groups(a)[2 + d])], yrec[a].at[d, step],
+                y_send.at[a, d, step], y_recv.at[a, d, step], y_peer,
             )
-
-    def y_add(a, k):
-        cols = pl.ds(2 * CA[a], 2 * CB[a])
-        for j in (2 * k, 2 * k + 1):
-            ys[a, j].wait_recv()
-            own[a, pl.ds(j * 32 + 16, 16), cols] += yrec[a][j]
 
     def ring_a(a, step):
         for d in range(2):
@@ -168,9 +161,12 @@
     def ring_b(a, step):
         for d in range(2):
             where = (a, pl.ds(slot_of(d, step) * 32 + 16, 16), pl.ds(*groups(a)[2 + d]))
+            ys[a, d, step].wait_recv()
             if step:
                 rings_b[a, d, step - 1].wait_recv()
-                own[where] += brec[a][d, step - 1]
+                own[where] += yrec[a][d, step] + brec[a][d, step - 1]
+            else:
+                own[where] += yrec[a][d, step]
             if step < NZ - 1:
                 rings_b[a, d, step] = remote(
                     own.at[where], brec[a].at[d, step], b_send.at[a, d, step], b_recv.at[a, d, step], z_next[d]
@@ -233,7 +229,7 @@
             tok[rows, :] = (part * inverse * gain[...]).astype(BF16)
             return carry
 
-        lax.fori_loop(0, 8, some, 0, unroll=2)
+        lax.fori_loop(0, 8, some, 0, unroll=8)
 
     def front(k):
         if k == 0:
@@ -302,31 +298,29 @@
     pl.semaphore_wait(barrier, 7)
     mix(0)
     back(0)
+    norm(1)
     pair_add(0, 0)
+    ring_a(0, 0)
     y_start(0, 0)
-    ring_a(0, 0)
-    norm(1)
+    front(1)
     pair_add(1, 0)
+    ring_a(1, 0)
     y_start(1, 0)
-    ring_a(1, 0)
-    front(1)
     mix(1)
     norm(2)
-    norm(3)
-    pair_add(0, 1)
-    y_start(0, 1)
-    ring_a(0, 1)
-    y_add(0, 0)
-    ring_b(0, 0)
     front(2)
     mix(2)
+    pair_add(0, 1)
+    ring_a(0, 1)
+    y_start(0, 1)
+    ring_b(0, 0)
+    norm(3)
     front(3)
     pair_add(0, 2)
-    ring_a(0, 2)
     y_start(0, 2)
-    y_add(1, 0)
     ring_b(1, 0)
     mix(3)
+    ring_a(0, 2)
     grad(0)
     grad(1)
     x_step(0)
@@ -334,54 +328,56 @@
     grad(3)
     grad(4)
     grad(5)
+    grad(6)
+    grad(7)
+    ring_b(0, 1)
     pair_add(0, 3)
     y_start(0, 3)
+    y_start(0, 4)
+    y_start(0, 5)
+    back(1)
     ring_a(0, 3)
-    y_add(0, 1)
-    ring_b(0, 1)
-    grad(6)
-    grad(7)
-    back(1)
-    ring_a(0, 4)
-    y_add(0, 2)
+    back(2)
     pair_add(1, 1)
+    ring_a(1, 1)
     y_start(1, 1)
     ring_b(0, 2)
-    ring_a(1, 1)
-    back(2)
+    y_start(0, 6)
+    back(3)
+    ring_a(0, 4)
     x_step(1)
-    ring_a(0, 5)
-    y_add(0, 3)
-    ring_b(0, 3)
     pair_add(1, 2)
+    ring_a(1, 2)
     y_start(1, 2)
-    back(3)
-    ring_a(1, 2)
-    ring_a(0, 6)
     pair_add(1, 3)
     y_start(1, 3)
+    y_start(1, 4)
+    ring_b(0, 3)
+    y_start(0, 7)
+    ring_b(1, 1)
+    y_start(1, 5)
+    ring_a(0, 5)
+    ring_a(1, 3)
     ring_b(0, 4)
-    y_add(1, 1)
-    ring_b(1, 1)
-    ring_a(1, 3)
+    ring_b(1, 2)
+    y_start(1, 6)
     x_step(2)
-    final_start(0)
-    ring_b(0, 5)
-    y_add(1, 2)
-    ring_b(1, 2)
+    ring_a(0, 6)
     drain()
     ring_a(1, 4)
-    ring_b(0, 6)
-    y_add(1, 3)
+    ring_b(0, 5)
     ring_b(1, 3)
+    y_start(1, 7)
+    final_start(0)
     drain()
     ring_a(1, 5)
     x_step(3)
-    ring_b(0, 7)
-    final_add(0)
+    ring_b(0, 6)
     ring_b(1, 4)
     drain()
     ring_a(1, 6)
+    ring_b(0, 7)
+    final_add(0)
     ring_b(1, 5)
     drain()
     final_start(1)
@@ -443,12 +439,12 @@
             v((2, 256, D), F32), v((2, 256, D), F32), v((2, 256, D), F32), v((8, units, cols), F32),
             v((2, 7, 32, CA[0]), F32), v((2, 7, 32, CA[1]), F32),
             v((2, 7, 16, CB[0]), F32), v((2, 7, 16, CB[1]), F32),
-            v((8, 16, 2 * CB[0]), F32), v((8, 16, 2 * CB[1]), F32),
+            v((2, 8, 16, CB[0]), F32), v((2, 8, 16, CB[1]), F32),
             v((16, 2 * CA[0]), F32), v((16, 2 * CA[1]), F32),
             v((2, 3, units, cols), F32), v((units, cols), F32),
             dma((7,)), dma((4,)), dma((4,)), dma((4,)),
             dma((2, 4, 4)), dma((2, 4, 4)), dma((2, 2, 7)), dma((2, 2, 7)), dma((2, 2, 7)), dma((2, 2, 7)),
-            dma((2, 8)), dma((2, 8)), dma((2, 2)), dma((2, 3)), dma((2, 3)), dma((2,)),
+            dma((2, 2, 8)), dma((2, 2, 8)), dma((2, 2)), dma((2, 3)), dma((2, 3)), dma((2,)),
         ],
         compiler_params=pltpu.CompilerParams(
             collective_id=0, has_side_effects=True, vmem_limit_bytes=63 * 2**20

time: 88 us -> 85.7 us (0.974)
  Pallas kernels: 87.1 us -> 84.8 us
    pallas_call x1, Pallas kernels: 85 us -> 82.6 us  [body(): pl.pallas_call(kernel, name='window', out_shape=results, in_specs=[hbm] *...]
where the time goes in v3:
time: 85.7 us; the launch traced here: 85.6 us
  Pallas kernels  84.8 us (99%)
    pallas_call x1, Pallas kernels, body(): pl.pallas_call(kernel, name='window', out_shape=results, in_specs=[hbm] *...  82.6 us
    pallas_call x1, Pallas kernels, body(): pl.pallas_call(hand_on, name='hand_on', out_shape=results, in_specs=[hbm]...  2.14 us

profile of v3, /device:TPU:2, one launch (start us, length us, event | category | flops | bytes accessed | tf_op | source)
XLA Modules:
  0.0 85.6 jit_solution(9291201517884701371)
XLA Ops:
  0.6 82.6 %window.1 = (bf16[16,4096]{1,0:T(8,128)(2,1)}, bf16[16,4096]{1,0:T(8,128)(2,1)}, f32[224,512]{1,0:T(8,128)}, f32[224,512]{1,0:T(8,128)}) custom-call(bf16[512,4096]{1,0:T(8,128)(2,1)} %tokens.1, f32[1,4096]{1,0:T(1,128)} %bitcast.5, bf16[1,224,4096]{2,1,0:T(8,128)(2,1)} %bitcast.3, bf16[1,224,4096]{2,1,0:T(8,128)(2,1)} %bitcast.4, ...), custom_call_target="tpu_custom_call" | custom-call | tf_op jit(solution)/shard_map/window/pallas_call | solution.py:428
  83.3 2.1 %hand_on.1 = (bf16[16,4096]{1,0:T(8,128)(2,1)}, bf16[16,4096]{1,0:T(8,128)(2,1)}, f32[224,512]{1,0:T(8,128)}, f32[224,512]{1,0:T(8,128)}) custom-call(bf16[16,4096]{1,0:T(8,128)(2,1)} %get-tuple-element.8.refs_0_, bf16[16,4096]{1,0:T(8,128)(2,1)} %get-tuple-element.9.refs_1_, f32[224,512]{1,0:T(8,128)} %get-tuple-element.10.refs_2_, ...), custom_call_target="tpu_custom_call" | custom-call | tf_op jit(solution)/shard_map/hand_on/pallas_call | solution.py:456

commit v4 on v3

--- a/solution.py
+++ b/solution.py
@@ -92,15 +92,14 @@
     ]
     loads[0].start()
     load_rows(tokens, tok, tok_sem, 0)
-    for i in (1, 2):
+    for i in (1, 2, 3):
         loads[i].start()
+    load_rows(tokens, tok, tok_sem, 1)
 
     barrier = pltpu.get_barrier_semaphore()
     for other in (pair, *z_next, y_peer, *x_next, l_peer):
         pl.semaphore_signal(barrier, inc=1, device_id=other, device_id_type=MESH)
 
-    loads[3].start()
-    load_rows(tokens, tok, tok_sem, 1)
     load_rows(cot_hbm, cot, cot_sem, 0)
     for k in (2, 3):
         load_rows(tokens, tok, tok_sem, k)

time: 85.7 us -> 84.9 us (level)
  no operation moved by 1% of the time
where the time goes in v4:
time: 84.9 us; the launch traced here: 84.8 us
  Pallas kernels  84 us (99%)
    pallas_call x1, Pallas kernels, body(): pl.pallas_call(kernel, name='window', out_shape=results, in_specs=[hbm] *...  81.9 us
    pallas_call x1, Pallas kernels, body(): pl.pallas_call(hand_on, name='hand_on', out_shape=results, in_specs=[hbm]...  2.14 us

profile of v4, /device:TPU:2, one launch (start us, length us, event | category | flops | bytes accessed | tf_op | source)
XLA Modules:
  0.0 84.8 jit_solution(117998085314554967)
XLA Ops:
  0.6 81.9 %window.1 = (bf16[16,4096]{1,0:T(8,128)(2,1)}, bf16[16,4096]{1,0:T(8,128)(2,1)}, f32[224,512]{1,0:T(8,128)}, f32[224,512]{1,0:T(8,128)}) custom-call(bf16[512,4096]{1,0:T(8,128)(2,1)} %tokens.1, f32[1,4096]{1,0:T(1,128)} %bitcast.5, bf16[1,224,4096]{2,1,0:T(8,128)(2,1)} %bitcast.3, bf16[1,224,4096]{2,1,0:T(8,128)(2,1)} %bitcast.4, ...), custom_call_target="tpu_custom_call" | custom-call | tf_op jit(solution)/shard_map/window/pallas_call | solution.py:427
  82.5 2.1 %hand_on.1 = (bf16[16,4096]{1,0:T(8,128)(2,1)}, bf16[16,4096]{1,0:T(8,128)(2,1)}, f32[224,512]{1,0:T(8,128)}, f32[224,512]{1,0:T(8,128)}) custom-call(bf16[16,4096]{1,0:T(8,128)(2,1)} %get-tuple-element.8.refs_0_, bf16[16,4096]{1,0:T(8,128)(2,1)} %get-tuple-element.9.refs_1_, f32[224,512]{1,0:T(8,128)} %get-tuple-element.10.refs_2_, ...), custom_call_target="tpu_custom_call" | custom-call | tf_op jit(solution)/shard_map/hand_on/pallas_call | solution.py:455
